TPU v7x, 32 devices: a whole 2x2x4 slice. The times are simulated.
32 devices in a mesh: row: 4 (over z), col: 8 (over y, x, core).
Axes of the slice: x: 2, y: 2, z: 4, core: 2. Of those that a mesh axis runs over, the one named last changes fastest.
Arguments:
- pair_counts: float32 [32, 32, 2, 128, 128], P(('row', 'col')), may hold values from 0.01 to 30
- tile_index: int32 [32, 32, 2], P(('row', 'col')), may hold values from 0 to 255
- slot_counts: int32 [32, 32], P(('row', 'col')), may hold values from 0 to 2, as said below
- row_totals: int32 [8192], P('row'), may hold values from 1000 to 59999
- col_totals: int32 [16384], P('col'), may hold values from 1000 to 59999
- sketch: bfloat16 [16384, 128], P('col'), may hold values from -0.046875 to 0.046875
Outputs:
- range_rows: bfloat16 [8192, 128], P('row')
- corange: bfloat16 [16384, 128], P('col')
Inputs may be any that keep to these rules, and one draw needn't show every extreme that they name: `slot_counts`: slot counts from a shard to an owner; for some owners every shard fills all 2 slots. `tile_index`: tile positions may repeat; repeated tiles add.
All inputs are finite; a program needn't handle non-finite values.
Results may differ from a plain program's by a relative error of at most 0.001.
The roundings to bfloat16 on the way count: a program that leaves them out, or rounds other values in their place, can miss the bound.
Values may be sent and summed in bfloat16 or wider, within the bound.
A program may use at most 128 MiB of HBM per device.

v0:
```python
import math

import jax
import jax.numpy as jnp
from jax import lax
from jax.sharding import PartitionSpec as P

TILE = 128
RT_DEV = 16
CT_DEV = 16


log_shift = 0.25


def pmi_block(tiles, parked, row_here, col_here, grand):
    ntiles = RT_DEV * CT_DEV
    stack = jnp.zeros((ntiles + 1, TILE, TILE), jnp.float32).at[parked].add(tiles)[:ntiles]
    counts_block = (
        stack.reshape(RT_DEV, CT_DEV, TILE, TILE)
        .transpose(0, 2, 1, 3)
        .reshape(RT_DEV * TILE, CT_DEV * TILE)
    )
    scaled = (
        counts_block
        * grand
        / (row_here.astype(jnp.float32)[:, None] * col_here.astype(jnp.float32)[None, :])
    )
    return jnp.maximum(jnp.log1p(scaled) - log_shift, 0.0).astype(jnp.bfloat16)


def on_device(pair_counts, tile_index, slot_counts, row_totals, col_totals, sketch):
    row_count = lax.axis_size("row")
    slots = lax.broadcasted_iota(jnp.int32, tile_index.shape, 2)
    parked = jnp.where(slots < slot_counts[:, :, None], tile_index, RT_DEV * CT_DEV)
    grand = lax.psum(jnp.sum(row_totals.astype(jnp.float32)), "row")
    arrived, places = (
        lax.all_to_all(pair_counts, ("row", "col"), split_axis=1, concat_axis=0, tiled=True),
        lax.all_to_all(parked, ("row", "col"), split_axis=1, concat_axis=0, tiled=True),
    )
    pmi = pmi_block(
        arrived.reshape(-1, TILE, TILE), places.reshape(-1), row_totals, col_totals, grand
    )
    partial_rows = jnp.dot(pmi, sketch, preferred_element_type=jnp.float32)
    range_rows = lax.psum(partial_rows, "col").astype(jnp.bfloat16)
    partial_cols = lax.dot_general(
        pmi, range_rows, (((0,), (0,)), ((), ())), preferred_element_type=jnp.float32
    )
    col_sums = lax.psum(partial_cols, "row")
    total_rows = pmi.shape[0] * row_count
    corange = (col_sums / math.sqrt(total_rows)).astype(jnp.bfloat16)
    return (range_rows, corange)


def solution(mesh):
    placed = (
        P(("row", "col"), None, None, None, None),
        P(("row", "col"), None, None),
        P(("row", "col"), None),
        P("row"),
        P("col"),
        P("col", None),
    )
    return jax.shard_map(
        on_device,
        mesh=mesh,
        in_specs=placed,
        out_specs=(P("row", None), P("col", None)),
        check_vma=False,
    )
```

profile of v0, /device:TPU:0, one launch (start us, length us, event | category | flops | bytes accessed | tf_op | source)
XLA Modules:
  0.0 312.3 jit_solution(12001681732545011220)
XLA Ops:
  7.2 0.0 copy-start
  7.2 0.7 compare_select_fusion.1
  7.9 0.1 copy.17
  8.0 14.2 %all_to_all.8 = s32[1,32,2]{2,0,1:T(1,128)S(1)} all-to-all(s32[1,32,2]{2,0,1:T(1,128)S(1)} %copy.17), channel_id=1, replica_groups=mesh['row'=4,'col'=8] {'row','col'}, dimensions={1} | all-to-all | bytes 512 | tf_op jit(solution)/shard_map/all_to_all | solution.py:39
  22.3 3.6 %all-to-all-start.1 = ((f32[1,32,2,128,128]{4,3,2,0,1:T(8,128)}), f32[1,32,2,128,128]{4,3,2,0,1:T(8,128)}, u32[]{:S(2)}, u32[]{:S(2)}) async-start(f32[1,32,2,128,128]{4,3,2,0,1:T(8,128)} %bitcast.27), calls=%async_computation.1 | async-start | bytes 8388608 | tf_op jit(solution)/shard_map/all_to_all | solution.py:38
  25.8 0.0 all-reduce.3.cloned.1.call-start
  25.9 1.3 convert_reduce_fusion
  27.2 74.1 %psum.21 = f32[]{:T(128)} all-reduce(f32[]{:T(128)} %convert_reduce_fusion), channel_id=1, replica_groups=mesh['row'=4,'col'=8] {'row'}, use_global_device_ids=true, to_apply=%region_2.3 | all-reduce | flops 1 | bytes 8 | tf_op jit(solution)/shard_map/psum | solution.py:36
  101.3 0.7 convert_element_type.16
  102.0 0.7 convert_element_type.17
  102.7 0.5 broadcast.52
  103.2 0.7 reduce.3
  103.9 0.1 reshape.89
  104.0 16.0 %all-to-all-done.1 = f32[1,32,2,128,128]{4,3,2,0,1:T(8,128)} async-done(((f32[1,32,2,128,128]{4,3,2,0,1:T(8,128)}), f32[1,32,2,128,128]{4,3,2,0,1:T(8,128)}, u32[]{:S(2)}, u32[]{:S(2)}) %all-to-all-start.1) | async-done | bytes 4194336 | tf_op jit(solution)/shard_map/all_to_all | solution.py:38
  120.1 7.9 %broadcast_in_dim.6 = f32[257,128,128]{2,1,0:T(8,128)} broadcast(f32[]{:T(128)} %constant.6.clone.1), dimensions={} | broadcast | bytes 16842756 | tf_op jit(solution)/shard_map/broadcast_in_dim | solution.py:18
  128.0 13.7 %scatter_fusion = f32[257,128,128]{2,1,0:T(8,128)} fusion(f32[257,128,128]{2,1,0:T(8,128)} %broadcast_in_dim.6, s32[64]{0:T(128)S(1)} %fusion.4, f32[64,128,128]{2,1,0:T(8,128)} %bitcast.3), kind=kCustom, calls=%fused_computation | custom fusion | flops 1048576 | bytes 12583168 | tf_op jit(solution)/shard_map/scatter-add | solution.py:18
  141.6 7.2 %slice_multiply_fusion = f32[256,128,128]{2,1,0:T(8,128)S(1)} fusion(f32[257,128,128]{2,1,0:T(8,128)} %scatter_fusion, f32[]{:T(128)} %psum.21), kind=kLoop, calls=%fused_computation.5 | loop fusion | flops 4194304 | bytes 33554436 | tf_op jit(solution)/shard_map/mul | solution.py:25
  148.8 21.4 %copy.19 = f32[16,128,16,128]{3,2,1,0:T(8,128)S(1)} copy(f32[16,128,16,128]{3,1,2,0:T(8,128)S(1)} %bitcast.26) | data formatting | bytes 33554432 | tf_op jit(solution)/shard_map/mul | solution.py:25
  170.2 13.8 %fusion.3 = bf16[2048,2048]{1,0:T(8,128)(2,1)S(1)} fusion(f32[256,8,16,128]{3,2,1,0:T(8,128)S(1)} %bitcast.25, f32[2048]{0:T(1024)S(1)} %convert_element_type.17, f32[2048]{0:T(1024)S(1)} %convert_element_type.16), kind=kLoop, calls=%fused_computation.6 | loop fusion | flops 20971520 | bytes 25182208 | tf_op jit(solution)/shard_map/convert_element_type | solution.py:29
  184.1 0.0 copy-start.1
  184.1 3.2 %copy-done.1 = bf16[2048,2048]{1,0:T(8,128)(2,1)} copy-done((bf16[2048,2048]{1,0:T(8,128)(2,1)}, bf16[2048,2048]{1,0:T(8,128)(2,1)S(1)}, u32[]{:S(2)}) %copy-start.1) | copy-done | bytes 8388632
  187.3 0.0 copy-done
  187.3 2.3 fusion.5
  189.6 51.6 %all-reduce.4 = bf16[2048,128]{1,0:T(8,128)(2,1)S(1)} all-reduce(f32[2048,128]{1,0:T(8,128)S(1)} %fusion.5), channel_id=1, replica_groups=mesh['row'=4,'col'=8] {'col'}, use_global_device_ids=true, to_apply=%region_3.4 | all-reduce | flops 262144 | bytes 1572864 | tf_op jit(solution)/shard_map/psum | solution.py:45
  241.3 0.0 copy-start.2
  241.3 7.0 %fusion.6 = f32[2048,128]{1,0:T(8,128)} fusion(bf16[2048,2048]{1,0:T(8,128)(2,1)} %copy-done.1, bf16[2048,128]{1,0:T(8,128)(2,1)S(1)} %all-reduce.4), kind=kOutput, calls=%fused_computation.13 | convolution fusion | flops 1073741824 | bytes 9961472 | tf_op jit(solution)/shard_map/dot_general | solution.py:46
  248.3 0.0 all-reduce.3.cloned.1.call-update
  248.3 55.0 %all-reduce.3.cloned.1.call-done = f32[2048,128]{1,0:T(8,128)} async-done(((f32[2048,128]{1,0:T(8,128)}), f32[2048,128]{1,0:T(8,128)}) %all-reduce.3.cloned.1.call-update) | async-done | bytes 1048592 | tf_op jit(solution)/shard_map/psum | solution.py:49
  303.3 2.1 multiply_convert_fusion
  305.4 0.0 copy-done.2
  (1 shorter events, 0.0 us)
Async XLA Ops:
  7.2 180.1 %copy-start = (bf16[2048,128]{1,0:T(8,128)(2,1)S(1)}, bf16[2048,128]{1,0:T(8,128)(2,1)}, u32[]{:S(2)}) copy-start(bf16[2048,128]{1,0:T(8,128)(2,1)} %param.11) | copy-start | bytes 1572868
  22.3 97.8 %all-to-all-start.1 = ((f32[1,32,2,128,128]{4,3,2,0,1:T(8,128)}), f32[1,32,2,128,128]{4,3,2,0,1:T(8,128)}, u32[]{:S(2)}, u32[]{:S(2)}) async-start(f32[1,32,2,128,128]{4,3,2,0,1:T(8,128)} %bitcast.27), calls=%async_computation.1 | async-start | bytes 8388608 | tf_op jit(solution)/shard_map/all_to_all | solution.py:38
  25.8 277.5 %all-reduce.3.cloned.1.call-start = ((), (), s32[]{:S(2)}) async-start(), calls=%async_computation.2 | async-start | bytes 2097152 | tf_op jit(solution)/shard_map/psum | solution.py:49
  184.1 3.2 %copy-start.1 = (bf16[2048,2048]{1,0:T(8,128)(2,1)}, bf16[2048,2048]{1,0:T(8,128)(2,1)S(1)}, u32[]{:S(2)}) copy-start(bf16[2048,2048]{1,0:T(8,128)(2,1)S(1)} %fusion.3) | copy-start | bytes 25165828
  241.3 64.1 %copy-start.2 = (bf16[2048,128]{1,0:T(8,128)(2,1)}, bf16[2048,128]{1,0:T(8,128)(2,1)S(1)}, u32[]{:S(2)}) copy-start(bf16[2048,128]{1,0:T(8,128)(2,1)S(1)} %all-reduce.4) | copy-start | bytes 1572868
Sparse Core Ops, SparseCore 0:
  248.5 54.8 all-reduce.2
where the time goes:
time: 313 us; the launch traced here: 312 us
  blocking collectives  140 us (45%)
  waiting for transfers between devices  71 us (23%)
  other arithmetic  40.9 us (13%)
  local copies, waits for them, and re-layouts  33.2 us (11%)
  between operations  14.1 us (5%)
  matrix products  9.36 us (3%)
  starting transfers between devices  3.63 us (1%)
    psum x1, blocking collectives, on_device(): grand = lax.psum(jnp.sum(row_totals.astype(jnp.float32)), 'row')  74.1 us
    psum x1, waiting for transfers between devices, on_device(): col_sums = lax.psum(partial_cols, 'row')  55 us
    psum x1, blocking collectives, on_device(): range_rows = lax.psum(partial_rows, 'col').astype(jnp.bfloat16)  51.6 us
    mul x1, local copies, waits for them, and re-layouts, pmi_block(): counts_block * grand  21.4 us
    all_to_all x1, waiting for transfers between devices, on_device(): lax.all_to_all(pair_counts, ('row', 'col'), split_axis=1, concat_axis=0,...  16 us
    all_to_all x1, blocking collectives, on_device(): lax.all_to_all(parked, ('row', 'col'), split_axis=1, concat_axis=0, tiled...  14.2 us
    convert_element_type x1, other arithmetic, pmi_block(): return jnp.maximum(jnp.log1p(scaled) - log_shift, 0.0).astype(jnp.bfloat16)  13.8 us
    scatter-add x1, other arithmetic, pmi_block(): jnp.zeros((ntiles + 1, TILE, TILE), jnp.float32).at[parked].add(tiles)  13.7 us
  transfers between devices with their start and end apart: 2, of which 2 were waited for; matrix products, arithmetic and copies ran while one was open for 1% of the time, Pallas kernels for 0%

commit v1 on v0

v1 whole, which is shorter than its diff:
```python
import functools
import math

import jax
import jax.numpy as jnp
from jax import lax
from jax.experimental import pallas as pl
from jax.experimental.pallas import tpu as pltpu
from jax.sharding import PartitionSpec as P

TILE = 128
RT_DEV = 16
CT_DEV = 16
NT = RT_DEV * CT_DEV
SHIFT = 0.25
SCALE = 2.0**19
MESH = pl.DeviceIdType.MESH
VLIM = 56 * 1024 * 1024


def exchange_kernel(nr, nc, counts, meta, words_out, meta_out, send, sem_s, sem_r, msem_s, msem_r, lsem):
    n = nr * nc
    me = lax.axis_index("row") * nc + lax.axis_index("col")

    def pack(o):
        low = None
        for h in range(2):
            v = jnp.round(counts[o, h] * SCALE).astype(jnp.int32)
            send[o, h] = ((v >> 8) - 32768).astype(jnp.int16)
            part = v & 255
            low = part if h == 0 else low + (part << 8)
        send[o, 2] = (low - 32768).astype(jnp.int16)

    def copies(d):
        o = lax.rem(me + d, n)
        to = (o // nc, lax.rem(o, nc))
        return (
            pltpu.make_async_remote_copy(
                src_ref=send.at[o], dst_ref=words_out.at[me], send_sem=sem_s.at[d],
                recv_sem=sem_r.at[d], device_id=to, device_id_type=MESH),
            pltpu.make_async_remote_copy(
                src_ref=meta.at[o], dst_ref=meta_out.at[me], send_sem=msem_s.at[d],
                recv_sem=msem_r.at[d], device_id=to, device_id_type=MESH),
        )

    def issue(i, _):
        d = i + 1
        pack(lax.rem(me + d, n))
        a, b = copies(d)
        a.start()
        b.start()
        return 0

    lax.fori_loop(0, n - 1, issue, 0)
    pack(me)
    own = pltpu.make_async_copy(send.at[me], words_out.at[me], lsem.at[0])
    own_meta = pltpu.make_async_copy(meta.at[me], meta_out.at[me], lsem.at[1])
    own.start()
    own_meta.start()

    def finish(i, _):
        a, b = copies(i + 1)
        a.wait()
        b.wait()
        return 0

    lax.fori_loop(0, n - 1, finish, 0)
    own.wait()
    own_meta.wait()


def pmi_kernel(nr, nc, meta, words, row_tot, col_tot, out, acc, row_f, col_f, seen):
    n = nr * nc

    def clear(i, _):
        seen[i] = 0
        return 0

    lax.fori_loop(0, NT, clear, 0)
    total = lax.fori_loop(0, nr, lambda a, t: t + meta[a * nc * 3 + 2], jnp.int32(0))
    grand = total.astype(jnp.float32)
    col_f[...] = (1.0 / SCALE) / col_tot[...].astype(jnp.float32)

    def rows(i, _):
        r = row_tot[pl.ds(i, 1), :].astype(jnp.float32)
        f = jnp.broadcast_to(grand / r, (TILE, TILE))
        row_f[pl.ds(i * TILE, TILE), :] = f.T
        return 0

    lax.fori_loop(0, RT_DEV, rows, 0)

    def add(s, _):
        for h in range(2):
            p = meta[s * 3 + h]

            @pl.when(p < NT)
            def _():
                low = words[s, 2].astype(jnp.int32) + 32768
                low = (low & 255) if h == 0 else (low >> 8)
                v = (words[s, h].astype(jnp.int32) + 32768) * 256 + low
                before = seen[p]

                @pl.when(before == 0)
                def _():
                    acc[p] = v

                @pl.when(before != 0)
                def _():
                    acc[p] = acc[p] + v

                seen[p] = 1

        return 0

    lax.fori_loop(0, n, add, 0)

    def tile(p, _):
        tr = p // CT_DEV
        tc = lax.rem(p, CT_DEV)
        rs = pl.ds(pl.multiple_of(tr * TILE, TILE), TILE)
        cs = pl.ds(pl.multiple_of(tc * TILE, TILE), TILE)

        @pl.when(seen[p] == 0)
        def _():
            out[rs, cs] = jnp.zeros((TILE, TILE), jnp.bfloat16)

        @pl.when(seen[p] != 0)
        def _():
            x = acc[p].astype(jnp.float32) * row_f[rs, :] * col_f[pl.ds(tc, 1), :]
            out[rs, cs] = jnp.maximum(jnp.log1p(x) - SHIFT, 0.0).astype(jnp.bfloat16)

        return 0

    lax.fori_loop(0, NT, tile, 0)


def sketch_kernel(nr, nc, inv, pmi, sketch, rr_out, co_out, p1, r1, rr, acc, p2, r2, co,
                  s1s, s1r, s2s, s2r, s3s, s3r, s4s, s4r):
    my_r = lax.axis_index("row")
    my_c = lax.axis_index("col")
    ch = pmi.shape[0] // nc
    cz = pmi.shape[1] // nr

    def rows_of(j):
        return pl.ds(pl.multiple_of(j * ch, ch), ch)

    def cols_of(j):
        return pl.ds(pl.multiple_of(j * cz, cz), cz)

    def rs_col(d):
        return pltpu.make_async_remote_copy(
            src_ref=p1.at[d], dst_ref=r1.at[d], send_sem=s1s.at[d], recv_sem=s1r.at[d],
            device_id=(my_r, lax.rem(my_c + d, nc)), device_id_type=MESH)

    def ag_col(d):
        return pltpu.make_async_remote_copy(
            src_ref=rr.at[rows_of(my_c)], dst_ref=rr.at[rows_of(my_c)], send_sem=s2s.at[d],
            recv_sem=s2r.at[d], device_id=(my_r, lax.rem(my_c + d, nc)), device_id_type=MESH)

    def rs_row(d):
        return pltpu.make_async_remote_copy(
            src_ref=p2.at[d], dst_ref=r2.at[d], send_sem=s3s.at[d], recv_sem=s3r.at[d],
            device_id=(lax.rem(my_r + d, nr), my_c), device_id_type=MESH)

    def ag_row(d):
        return pltpu.make_async_remote_copy(
            src_ref=co.at[cols_of(my_r)], dst_ref=co.at[cols_of(my_r)], send_sem=s4s.at[d],
            recv_sem=s4r.at[d], device_id=(lax.rem(my_r + d, nr), my_c), device_id_type=MESH)

    def product(j):
        return jnp.dot(pmi[rows_of(j), :], sketch[...], preferred_element_type=jnp.float32)

    def first(i, _):
        d = i + 1
        p1[d] = product(lax.rem(my_c + d, nc))
        rs_col(d).start()
        return 0

    lax.fori_loop(0, nc - 1, first, 0)
    p1[0] = product(my_c)

    def gather(i, _):
        rs_col(i + 1).wait()
        p1[0] = p1[0] + r1[i + 1]
        return 0

    lax.fori_loop(0, nc - 1, gather, 0)
    rr[rows_of(my_c), :] = p1[0].astype(jnp.bfloat16)

    def spread(i, _):
        ag_col(i + 1).start()
        return 0

    lax.fori_loop(0, nc - 1, spread, 0)

    def turned(j):
        left = rr[rows_of(j), :].astype(jnp.float32).T.astype(jnp.bfloat16)
        return jnp.dot(left, pmi[rows_of(j), :], preferred_element_type=jnp.float32)

    acc[...] = turned(my_c)

    def second(i, _):
        ag_col(i + 1).wait_recv()
        acc[...] += turned(lax.rem(my_c - (i + 1) + nc, nc))
        return 0

    lax.fori_loop(0, nc - 1, second, 0)

    def third(i, _):
        d = i + 1
        p2[d] = acc[:, cols_of(lax.rem(my_r + d, nr))].T
        rs_row(d).start()
        return 0

    lax.fori_loop(0, nr - 1, third, 0)
    p2[0] = acc[:, cols_of(my_r)].T

    def sent(i, _):
        ag_col(i + 1).wait_send()
        return 0

    lax.fori_loop(0, nc - 1, sent, 0)
    rr_out[...] = rr[...]

    def fourth(i, _):
        rs_row(i + 1).wait()
        p2[0] = p2[0] + r2[i + 1]
        return 0

    lax.fori_loop(0, nr - 1, fourth, 0)
    co[cols_of(my_r), :] = (p2[0] * inv).astype(jnp.bfloat16)

    def fifth(i, _):
        ag_row(i + 1).start()
        return 0

    lax.fori_loop(0, nr - 1, fifth, 0)

    def sixth(i, _):
        ag_row(i + 1).wait()
        return 0

    lax.fori_loop(0, nr - 1, sixth, 0)
    co_out[...] = co[...]


def on_device(nr, nc, pair_counts, tile_index, slot_counts, row_totals, col_totals, sketch):
    n = nr * nc
    vm = pl.BlockSpec(memory_space=pltpu.VMEM)
    dma = pltpu.SemaphoreType.DMA
    slots = lax.broadcasted_iota(jnp.int32, tile_index.shape, 2)
    parked = jnp.where(slots < slot_counts[:, :, None], tile_index, NT)[0]
    part = jnp.broadcast_to(jnp.sum(row_totals), (n, 6))
    meta = jnp.concatenate([parked, part], axis=1)
    meta = jnp.broadcast_to(meta[:, :, None], (n, 8, TILE)).astype(jnp.int32)
    words, meta = pl.pallas_call(
        functools.partial(exchange_kernel, nr, nc),
        out_shape=(
            jax.ShapeDtypeStruct((n, 3, TILE, TILE), jnp.int16),
            jax.ShapeDtypeStruct((n, 8, TILE), jnp.int32),
        ),
        in_specs=[vm, vm],
        out_specs=(pl.BlockSpec(memory_space=pl.ANY), pl.BlockSpec(memory_space=pl.ANY)),
        scratch_shapes=[pltpu.VMEM((n, 3, TILE, TILE), jnp.int16)]
        + [dma((n,))] * 4 + [dma((2,))],
        compiler_params=pltpu.CompilerParams(has_side_effects=True, vmem_limit_bytes=VLIM),
        name="exchange",
    )(pair_counts[0], meta)
    pmi = pl.pallas_call(
        functools.partial(pmi_kernel, nr, nc),
        out_shape=jax.ShapeDtypeStruct((RT_DEV * TILE, CT_DEV * TILE), jnp.bfloat16),
        in_specs=[pl.BlockSpec(memory_space=pltpu.SMEM), vm, vm, vm],
        out_specs=vm,
        scratch_shapes=[
            pltpu.VMEM((NT, TILE, TILE), jnp.int32),
            pltpu.VMEM((RT_DEV * TILE, TILE), jnp.float32),
            pltpu.VMEM((CT_DEV, TILE), jnp.float32),
            pltpu.SMEM((NT,), jnp.int32),
        ],
        compiler_params=pltpu.CompilerParams(vmem_limit_bytes=VLIM),
        name="pmi",
    )(
        meta[:, :3, 0].reshape(-1),
        words,
        row_totals.reshape(RT_DEV, TILE),
        col_totals.reshape(CT_DEV, TILE),
    )
    rows, cols = pmi.shape
    sk = sketch.shape[1]
    ch, cz = rows // nc, cols // nr
    f32, bf16 = jnp.float32, jnp.bfloat16
    return pl.pallas_call(
        functools.partial(sketch_kernel, nr, nc, 1.0 / math.sqrt(rows * nr)),
        out_shape=(
            jax.ShapeDtypeStruct((rows, sk), bf16),
            jax.ShapeDtypeStruct((cols, sk), bf16),
        ),
        in_specs=[vm, vm],
        out_specs=(vm, vm),
        scratch_shapes=[
            pltpu.VMEM((nc, ch, sk), f32),
            pltpu.VMEM((nc, ch, sk), f32),
            pltpu.VMEM((rows, sk), bf16),
            pltpu.VMEM((sk, cols), f32),
            pltpu.VMEM((nr, cz, sk), f32),
            pltpu.VMEM((nr, cz, sk), f32),
            pltpu.VMEM((cols, sk), bf16),
        ]
        + [dma((nc,))] * 4 + [dma((nr,))] * 4,
        compiler_params=pltpu.CompilerParams(has_side_effects=True, vmem_limit_bytes=VLIM),
        name="sketch",
    )(pmi, sketch)


def solution(mesh):
    placed = (
        P(("row", "col"), None, None, None, None),
        P(("row", "col"), None, None),
        P(("row", "col"), None),
        P("row"),
        P("col"),
        P("col", None),
    )
    return jax.shard_map(
        functools.partial(on_device, mesh.shape["row"], mesh.shape["col"]),
        mesh=mesh,
        in_specs=placed,
        out_specs=(P("row", None), P("col", None)),
        check_vma=False,
    )
```

time: 313 us -> 192 us (0.61)
  Pallas kernels: 0 us -> 182 us
  blocking collectives: 140 us -> 0 us
  waiting for transfers between devices: 71 us -> 0 us
  other arithmetic: 40.9 us -> 2.02 us
  local copies, waits for them, and re-layouts: 33.2 us -> 7.37 us
  between operations: 14.1 us -> 0.66 us
  matrix products: 9.36 us -> 0 us
  starting transfers between devices: 3.63 us -> 0 us
    pallas_call x0 -> x3, Pallas kernels: none -> 182 us  [the longest x1 88.9 us: on_device(): pl.pallas_call(functools.partial(sketch_kernel, nr, nc, 1.0 / math.sqrt(r...]
    psum x2 -> x0, blocking collectives: 126 us -> none  [the longest x1 74.1 us: on_device(): grand = lax.psum(jnp.sum(row_totals.astype(jnp.float32)), 'row')]
    psum x1 -> x0, waiting for transfers between devices: 55 us -> none  [on_device(): col_sums = lax.psum(partial_cols, 'row')]
    mul x1 -> x0, local copies, waits for them, and re-layouts: 21.4 us -> none  [pmi_block(): counts_block * grand]
    convert_element_type x4 -> x0, other arithmetic: 17.3 us -> none  [the longest x1 13.8 us: pmi_block(): return jnp.maximum(jnp.log1p(scaled) - log_shift, 0.0).astype(jnp.bfloat16)]
    all_to_all x1 -> x0, waiting for transfers between devices: 16 us -> none  [on_device(): lax.all_to_all(pair_counts, ('row', 'col'), split_axis=1, concat_axis=0,...]
    all_to_all x1 -> x0, blocking collectives: 14.2 us -> none  [on_device(): lax.all_to_all(parked, ('row', 'col'), split_axis=1, concat_axis=0, tiled...]
    scatter-add x1 -> x0, other arithmetic: 13.7 us -> none  [pmi_block(): jnp.zeros((ntiles + 1, TILE, TILE), jnp.float32).at[parked].add(tiles)]
  transfers between devices with their start and end apart: 2 -> 0, of which waited for: 2 -> 0; matrix products, arithmetic and copies ran while one was open for 1% -> 0% of each run, Pallas kernels for 0% -> 0%
where the time goes in v1:
time: 192 us
  Pallas kernels  182 us (95%)
  local copies, waits for them, and re-layouts  7.37 us (4%)
  other arithmetic  2.02 us (1%)
    pallas_call x1, Pallas kernels, on_device(): pl.pallas_call(functools.partial(sketch_kernel, nr, nc, 1.0 / math.sqrt(r...  88.9 us
    pallas_call x1, Pallas kernels, on_device(): pl.pallas_call(functools.partial(exchange_kernel, nr, nc), out_shape=(jax...  74.7 us
    pallas_call x1, Pallas kernels, on_device(): pl.pallas_call(functools.partial(pmi_kernel, nr, nc), out_shape=jax.Shape...  18.3 us

profile of v1, /device:TPU:0, one launch (start us, length us, event | category | flops | bytes accessed | tf_op | source)
XLA Modules:
  0.0 191.9 jit_solution(8879441834513318813)
XLA Ops:
  0.6 1.3 reduce_sum.9
  2.0 0.7 fusion
  2.6 0.1 copy.10
  2.7 0.6 concatenate.3.clone
  3.4 0.8 broadcast_in_dim.7.meta
  4.2 74.7 %exchange.1 = (s16[32,3,128,128]{3,2,1,0:T(8,128)(2,1)}, s32[32,8,128]{2,1,0:T(8,128)}) custom-call(f32[32,2,128,128]{3,2,1,0:T(8,128)} %bitcast.6, s32[32,8,128]{2,1,0:T(8,128)} %broadcast_in_dim.7.meta), custom_call_target="tpu_custom_call" | custom-call | tf_op jit(solution)/shard_map/exchange/pallas_call | solution.py:256
  78.9 1.5 slice_reduce_fusion
  80.4 0.6 reshape_squeeze.3.meta
  81.0 18.3 %pmi.1 = bf16[2048,2048]{1,0:T(8,128)(2,1)} custom-call(s32[96]{0:T(128)} %reshape_squeeze.3.meta, s16[32,3,128,128]{3,2,1,0:T(8,128)(2,1)} %get-tuple-element.5.words, s32[16,128]{1,0:T(8,128)} %bitcast.7, s32[16,128]{1,0:T(8,128)} %bitcast.8), custom_call_target="tpu_custom_call" | custom-call | tf_op jit(solution)/shard_map/pmi/pallas_call | solution.py:269
  99.3 88.9 %sketch.2 = (bf16[2048,128]{1,0:T(8,128)(2,1)}, bf16[2048,128]{1,0:T(8,128)(2,1)}) custom-call(bf16[2048,2048]{1,0:T(8,128)(2,1)} %pmi.1, bf16[2048,128]{1,0:T(8,128)(2,1)} %sketch.3), custom_call_target="tpu_custom_call" | custom-call | tf_op jit(solution)/shard_map/sketch/pallas_call | solution.py:292
  188.2 1.9 copy.13
  190.0 1.9 copy.14

commit v2 on v1

v2 whole, which is shorter than its diff:
```python
import functools
import math

import jax
import jax.numpy as jnp
from jax import lax
from jax.experimental import pallas as pl
from jax.experimental.pallas import tpu as pltpu
from jax.sharding import PartitionSpec as P

TILE = 128
RT_DEV = 16
CT_DEV = 16
NT = RT_DEV * CT_DEV
HALF = TILE // 2
SHIFT = 0.25
CODE = 1048570.0 / math.sqrt(30.0)
TOP = 32766.0
MESH = pl.DeviceIdType.MESH
MIB = 1024 * 1024


def exchange_kernel(nr, nc, counts, places, used, row_tot, words_out, meta_out,
                    send, meta, sem_s, sem_r, msem_s, msem_r, lsem):
    n = nr * nc
    hr = nr // 2
    my_r = lax.axis_index("row")
    my_c = lax.axis_index("col")
    me = my_r * nc + my_c
    part = jnp.sum(row_tot[...])
    lane = lax.broadcasted_iota(jnp.int32, (1, TILE), 1)

    def pack(o):
        low = None
        for h in range(2):
            y = counts[o, h]
            r = lax.rsqrt(y)
            t = y * r
            t = t + 0.5 * r * (y - t * t)
            v = jnp.round(t * CODE).astype(jnp.int32)
            send[o, h * TILE : (h + 1) * TILE] = ((v >> 4) - 32768).astype(jnp.int16)
            v = v & 15
            v = v[:HALF] + (v[HALF:] << 4)
            low = v if h == 0 else low + (v << 8)
        send[o, 2 * TILE :] = (low - 32768).astype(jnp.int16)
        k = jnp.where(lane == 2, used[0, o], part)
        k = jnp.where(lane == 1, places[1, o], k)
        meta[o] = jnp.where(lane == 0, places[0, o], k)

    def target(i):
        q = i // 2
        side = lax.rem(my_r // hr + 1 + lax.rem(i, 2), 2)
        row = side * hr + lax.rem(my_r + q // nc, hr)
        return row, lax.rem(my_c + lax.rem(q, nc), nc)

    def copies(i):
        row, col = target(i)
        o = row * nc + col
        return o, (
            pltpu.make_async_remote_copy(
                src_ref=send.at[o], dst_ref=words_out.at[me], send_sem=sem_s.at[i],
                recv_sem=sem_r.at[i], device_id=(row, col), device_id_type=MESH),
            pltpu.make_async_remote_copy(
                src_ref=meta.at[o], dst_ref=meta_out.at[me], send_sem=msem_s.at[i],
                recv_sem=msem_r.at[i], device_id=(row, col), device_id_type=MESH),
        )

    def issue(i, _):
        o, (a, b) = copies(i)
        pack(o)
        a.start()
        b.start()
        return 0

    def finish(i, _):
        _, (a, b) = copies(i)
        a.wait()
        b.wait()
        return 0

    issue(0, 0)
    lax.fori_loop(2, n, issue, 0)
    pack(me)
    own = pltpu.make_async_copy(send.at[me], words_out.at[me], lsem.at[0])
    own_meta = pltpu.make_async_copy(meta.at[me], meta_out.at[me], lsem.at[1])
    own.start()
    own_meta.start()
    finish(0, 0)
    lax.fori_loop(2, n, finish, 0)
    own.wait()
    own_meta.wait()


def pmi_kernel(nr, nc, meta, words, row_tot, col_tot, out, acc, row_f, col_f, seen):
    n = nr * nc

    def clear(i, _):
        seen[i] = 0
        return 0

    lax.fori_loop(0, NT, clear, 0)
    total = lax.fori_loop(0, nr, lambda a, t: t + meta[a * nc, 0, 3], jnp.int32(0))
    grand = total.astype(jnp.float32)
    col_f[...] = (1.0 / (CODE * CODE)) / col_tot[...].astype(jnp.float32)

    def rows(i, _):
        r = row_tot[pl.ds(i, 1), :].astype(jnp.float32)
        f = jnp.broadcast_to(grand / r, (TILE, TILE))
        row_f[pl.ds(i * TILE, TILE), :] = f.T
        return 0

    lax.fori_loop(0, RT_DEV, rows, 0)

    def add(s, _):
        for h in range(2):
            p = meta[s, 0, h]

            @pl.when(h < meta[s, 0, 2])
            def _():
                low = (words[s, 2 * TILE :].astype(jnp.int32) + 32768) >> (8 * h)
                fresh = seen[p] == 0
                for g in range(2):
                    at = slice(g * HALF, (g + 1) * HALF)
                    from_ = slice(h * TILE + g * HALF, h * TILE + (g + 1) * HALF)
                    v = (words[s, from_].astype(jnp.int32) + 32768) * 16
                    v = (v + ((low >> (4 * g)) & 15)).astype(jnp.float32)
                    v = v * v

                    @pl.when(fresh)
                    def _():
                        acc[p, at] = v

                    @pl.when(jnp.logical_not(fresh))
                    def _():
                        acc[p, at] = acc[p, at] + v

                seen[p] = 1

        return 0

    lax.fori_loop(0, n, add, 0)

    def tile(p, _):
        tr = p // CT_DEV
        tc = lax.rem(p, CT_DEV)
        rs = pl.ds(pl.multiple_of(tr * TILE, TILE), TILE)
        cs = pl.ds(pl.multiple_of(tc * TILE, TILE), TILE)

        @pl.when(seen[p] == 0)
        def _():
            out[rs, cs] = jnp.zeros((TILE, TILE), jnp.bfloat16)

        @pl.when(seen[p] != 0)
        def _():
            x = acc[p] * row_f[rs, :] * col_f[pl.ds(tc, 1), :]
            out[rs, cs] = jnp.maximum(jnp.log(1.0 + x) - SHIFT, 0.0).astype(jnp.bfloat16)

        return 0

    lax.fori_loop(0, NT, tile, 0)


def sketch_kernel(nr, nc, inv, pmi, sketch, rr_out, co_out, pa, ra, p1, r1, rr, acc, p2, r2,
                  f2, g2, co, sas, sar, s1s, s1r, s2s, s2r, sfs, sfr, s3s, s3r, s5s, s5r,
                  s4s, s4r):
    my_r = lax.axis_index("row")
    my_c = lax.axis_index("col")
    nk = nc // 2
    k = my_c // 2
    core = lax.rem(my_c, 2)
    other = 1 - core
    ch = pmi.shape[0] // nc
    cz = pmi.shape[1] // nr

    def rows_of(j):
        return pl.ds(pl.multiple_of(j * ch, ch), ch)

    def cols_of(j):
        return pl.ds(pl.multiple_of(j * cz, cz), cz)

    def remote(src, dst, a, b, to):
        return pltpu.make_async_remote_copy(
            src_ref=src, dst_ref=dst, send_sem=a, recv_sem=b, device_id=to,
            device_id_type=MESH)

    sibling = (my_r, k * 2 + other)

    def chip(d):
        return (my_r, lax.rem(k + d, nk) * 2 + core)

    def to_sibling(d):
        return remote(pa.at[d], ra.at[d], sas.at[d], sar.at[d], sibling)

    def rs_col(d):
        return remote(p1.at[d], r1.at[d], s1s.at[d], s1r.at[d], chip(d))

    def ag_col(d):
        mine = rr.at[rows_of(my_c)]
        return remote(mine, mine, s2s.at[d], s2r.at[d], chip(d))

    def origin(d):
        return lax.rem(k - d + nk, nk) * 2

    def forward(d):
        block = rr.at[rows_of(origin(d) + core)]
        return remote(block, block, sfs.at[d], sfr.at[d], sibling)

    def row_peer(d):
        return (lax.rem(my_r + d, nr), my_c)

    def rs_row(d):
        return (
            remote(p2.at[d], r2.at[d], s3s.at[d], s3r.at[d], row_peer(d)),
            remote(f2.at[d], g2.at[d], s5s.at[d], s5r.at[d], row_peer(d)),
        )

    def ag_row(d):
        mine = co.at[cols_of(my_r)]
        return remote(mine, mine, s4s.at[d], s4r.at[d], row_peer(d))

    def product(j):
        return jnp.dot(pmi[rows_of(j), :], sketch[...], preferred_element_type=jnp.float32)

    def zeroth(i, _):
        d = lax.rem(i + 1, nk)
        pa[d] = product(lax.rem(k + d, nk) * 2 + other)
        to_sibling(d).start()
        return 0

    lax.fori_loop(0, nk, zeroth, 0)

    def first(i, _):
        d = i + 1
        mine = product(lax.rem(k + d, nk) * 2 + core)
        to_sibling(d).wait_recv()
        p1[d] = mine + ra[d]
        rs_col(d).start()
        return 0

    lax.fori_loop(0, nk - 1, first, 0)
    own = product(my_c)
    to_sibling(0).wait_recv()
    p1[0] = own + ra[0]

    def gather(i, _):
        rs_col(i + 1).wait_recv()
        p1[0] = p1[0] + r1[i + 1]
        return 0

    lax.fori_loop(0, nk - 1, gather, 0)
    rr[rows_of(my_c), :] = p1[0].astype(jnp.bfloat16)

    def spread(i, _):
        ag_col(i + 1).start()
        return 0

    lax.fori_loop(0, nk - 1, spread, 0)
    forward(0).start()

    def turned(j):
        left = rr[rows_of(j), :].astype(jnp.float32).T.astype(jnp.bfloat16)
        return jnp.dot(left, pmi[rows_of(j), :], preferred_element_type=jnp.float32)

    acc[...] = turned(my_c)
    forward(0).wait_recv()
    acc[...] += turned(k * 2 + other)

    def second(i, _):
        d = i + 1
        ag_col(d).wait_recv()
        forward(d).start()
        acc[...] += turned(origin(d) + core)
        forward(d).wait_recv()
        acc[...] += turned(origin(d) + other)
        return 0

    lax.fori_loop(0, nk - 1, second, 0)

    def third(i, _):
        d = i + 1
        a = acc[:, cols_of(lax.rem(my_r + d, nr))]
        m = jnp.max(jnp.abs(a), axis=0, keepdims=True)
        up = jnp.where(m > 1e-30, TOP / jnp.maximum(m, 1e-30), 0.0)
        p2[d] = jnp.round(a * up).astype(jnp.int32).astype(jnp.int16)
        f2[d] = jnp.broadcast_to(m * (1.0 / TOP), (8, cz))
        a, b = rs_row(d)
        a.start()
        b.start()
        return 0

    lax.fori_loop(0, nr - 1, third, 0)

    def sent(i, _):
        d = i + 1
        rs_col(d).wait_send()
        ag_col(d).wait_send()
        to_sibling(d).wait_send()
        forward(d).wait_send()
        return 0

    lax.fori_loop(0, nk - 1, sent, 0)
    to_sibling(0).wait_send()
    forward(0).wait_send()
    rr_out[...] = rr[...]
    mine = cols_of(my_r)

    def fourth(i, _):
        d = i + 1
        a, b = rs_row(d)
        a.wait()
        b.wait()
        acc[:, mine] += r2[d].astype(jnp.int32).astype(jnp.float32) * g2[d, 0:1, :]
        return 0

    lax.fori_loop(0, nr - 1, fourth, 0)
    co[mine, :] = (acc[:, mine].T * inv).astype(jnp.bfloat16)

    def fifth(i, _):
        ag_row(i + 1).start()
        return 0

    lax.fori_loop(0, nr - 1, fifth, 0)

    def sixth(i, _):
        ag_row(i + 1).wait()
        return 0

    lax.fori_loop(0, nr - 1, sixth, 0)
    co_out[...] = co[...]


def on_device(nr, nc, pair_counts, tile_index, slot_counts, row_totals, col_totals, sketch):
    n = nr * nc
    vm = pl.BlockSpec(memory_space=pltpu.VMEM)
    sm = pl.BlockSpec(memory_space=pltpu.SMEM)
    hbm = pl.BlockSpec(memory_space=pl.ANY)
    dma = pltpu.SemaphoreType.DMA
    f32, bf16, i16, i32 = jnp.float32, jnp.bfloat16, jnp.int16, jnp.int32
    row_tot = row_totals.reshape(RT_DEV, TILE)
    words_rows = 2 * TILE + HALF
    words, meta = pl.pallas_call(
        functools.partial(exchange_kernel, nr, nc),
        out_shape=(
            jax.ShapeDtypeStruct((n, words_rows, TILE), i16),
            jax.ShapeDtypeStruct((n, 1, TILE), i32),
        ),
        in_specs=[vm, sm, sm, vm],
        out_specs=(hbm, hbm),
        scratch_shapes=[pltpu.VMEM((n, words_rows, TILE), i16), pltpu.VMEM((n, 1, TILE), i32)]
        + [dma((n,))] * 4 + [dma((2,))],
        compiler_params=pltpu.CompilerParams(
            has_side_effects=True, vmem_limit_bytes=8 * MIB + n * MIB // 4),
        name="exchange",
    )(pair_counts[0], tile_index[0].T, slot_counts, row_tot)
    pmi = pl.pallas_call(
        functools.partial(pmi_kernel, nr, nc),
        out_shape=jax.ShapeDtypeStruct((RT_DEV * TILE, CT_DEV * TILE), bf16),
        in_specs=[sm, vm, vm, vm],
        out_specs=vm,
        scratch_shapes=[
            pltpu.VMEM((NT, TILE, TILE), f32),
            pltpu.VMEM((RT_DEV * TILE, TILE), f32),
            pltpu.VMEM((CT_DEV, TILE), f32),
            pltpu.SMEM((NT,), i32),
        ],
        compiler_params=pltpu.CompilerParams(vmem_limit_bytes=30 * MIB + n * MIB // 10),
        name="pmi",
    )(meta, words, row_tot, col_totals.reshape(CT_DEV, TILE))
    rows, cols = pmi.shape
    sk = sketch.shape[1]
    ch, cz, nk = rows // nc, cols // nr, nc // 2
    return pl.pallas_call(
        functools.partial(sketch_kernel, nr, nc, 1.0 / math.sqrt(rows * nr)),
        out_shape=(
            jax.ShapeDtypeStruct((rows, sk), bf16),
            jax.ShapeDtypeStruct((cols, sk), bf16),
        ),
        in_specs=[vm, vm],
        out_specs=(vm, vm),
        scratch_shapes=[pltpu.VMEM((nk, ch, sk), f32)] * 4
        + [
            pltpu.VMEM((rows, sk), bf16),
            pltpu.VMEM((sk, cols), f32),
            pltpu.VMEM((nr, sk, cz), i16),
            pltpu.VMEM((nr, sk, cz), i16),
            pltpu.VMEM((nr, 8, cz), f32),
            pltpu.VMEM((nr, 8, cz), f32),
            pltpu.VMEM((cols, sk), bf16),
        ]
        + [dma((nk,))] * 8 + [dma((nr,))] * 6,
        compiler_params=pltpu.CompilerParams(has_side_effects=True, vmem_limit_bytes=24 * MIB),
        name="sketch",
    )(pmi, sketch)


def solution(mesh):
    placed = (
        P(("row", "col"), None, None, None, None),
        P(("row", "col"), None, None),
        P(("row", "col"), None),
        P("row"),
        P("col"),
        P("col", None),
    )
    return jax.shard_map(
        functools.partial(on_device, mesh.shape["row"], mesh.shape["col"]),
        mesh=mesh,
        in_specs=placed,
        out_specs=(P("row", None), P("col", None)),
        check_vma=False,
    )
```

time: 192 us -> 139 us (0.72)
  Pallas kernels: 182 us -> 132 us
  other arithmetic: 2.02 us -> 0 us
    pallas_call x1, Pallas kernels: 88.9 us -> 62.3 us  [on_device(): pl.pallas_call(functools.partial(sketch_kernel, nr, nc, 1.0 / math.sqrt(r...]
    pallas_call x1, Pallas kernels: 74.7 us -> 55.8 us  [on_device(): pl.pallas_call(functools.partial(exchange_kernel, nr, nc), out_shape=(jax...]
    pallas_call x1, Pallas kernels: 18.3 us -> 13.5 us  [on_device(): pl.pallas_call(functools.partial(pmi_kernel, nr, nc), out_shape=jax.Shape...]
    unnamed x3 -> x16, local copies, waits for them, and re-layouts: 3.83 us -> 5.81 us
where the time goes in v2:
time: 139 us; the launch traced here: 138 us
  Pallas kernels  132 us (95%)
  local copies, waits for them, and re-layouts  5.81 us (4%)
    pallas_call x1, Pallas kernels, on_device(): pl.pallas_call(functools.partial(sketch_kernel, nr, nc, 1.0 / math.sqrt(r...  62.3 us
    pallas_call x1, Pallas kernels, on_device(): pl.pallas_call(functools.partial(exchange_kernel, nr, nc), out_shape=(jax...  55.8 us
    pallas_call x1, Pallas kernels, on_device(): pl.pallas_call(functools.partial(pmi_kernel, nr, nc), out_shape=jax.Shape...  13.5 us
    unnamed x16, local copies, waits for them, and re-layouts  5.81 us

profile of v2, /device:TPU:0, one launch (start us, length us, event | category | flops | bytes accessed | tf_op | source)
XLA Modules:
  0.0 138.1 jit_solution(1241328484503631653)
XLA Ops:
  0.6 0.0 copy-start
  0.6 2.2 %copy-done = f32[1,32,2,128,128]{4,3,2,1,0:T(8,128)S(1)} copy-done((f32[1,32,2,128,128]{4,3,2,1,0:T(8,128)S(1)}, f32[1,32,2,128,128]{4,3,2,1,0:T(8,128)}, u32[]{:S(2)}) %copy-start) | copy-done | bytes 4194328
  2.8 0.0 copy-start.2
  2.8 0.7 copy-done.2
  3.5 0.0 copy-start.5
  3.5 0.7 copy-done.5
  4.2 0.0 copy-start.6
  4.2 0.7 copy-done.6
  4.9 0.0 copy-start.3
  4.9 0.0 copy-start.4
  4.9 55.8 %exchange.1 = (s16[32,320,128]{2,1,0:T(8,128)(2,1)S(1)}, s32[32,1,128]{2,1,0:T(1,128)S(1)}) custom-call(f32[32,2,128,128]{3,2,1,0:T(8,128)S(1)} %bitcast.6, s32[2,32]{1,0:T(2,128)S(1)} %bitcast.10, s32[1,32]{1,0:T(1,128)S(1)} %copy-done.6, s32[16,128]{1,0:T(8,128)S(1)} %bitcast.7), custom_call_target="tpu_custom_call" | custom-call | tf_op jit(solution)/shard_map/exchange/pallas_call | solution.py:341
  60.6 0.0 copy-done.3
  60.6 0.0 copy-done.4
  60.6 0.0 copy-start.1
  60.7 13.5 %pmi.1 = bf16[2048,2048]{1,0:T(8,128)(2,1)S(1)} custom-call(s32[32,1,128]{2,1,0:T(1,128)S(1)} %get-tuple-element.4.meta, s16[32,320,128]{2,1,0:T(8,128)(2,1)S(1)} %get-tuple-element.5.words, s32[16,128]{1,0:T(8,128)S(1)} %bitcast.8, s32[16,128]{1,0:T(8,128)S(1)} %bitcast.9), custom_call_target="tpu_custom_call" | custom-call | tf_op jit(solution)/shard_map/pmi/pallas_call | solution.py:355
  74.2 0.0 copy-done.1
  74.2 62.3 %sketch.2 = (bf16[2048,128]{1,0:T(8,128)(2,1)S(1)}, bf16[2048,128]{1,0:T(8,128)(2,1)S(1)}) custom-call(bf16[2048,2048]{1,0:T(8,128)(2,1)S(1)} %pmi.1, bf16[2048,128]{1,0:T(8,128)(2,1)S(1)} %copy-done.1), custom_call_target="tpu_custom_call" | custom-call | tf_op jit(solution)/shard_map/sketch/pallas_call | solution.py:372
  136.5 0.8 copy.10
  137.3 0.8 copy.11
Async XLA Ops:
  0.6 2.2 %copy-start = (f32[1,32,2,128,128]{4,3,2,1,0:T(8,128)S(1)}, f32[1,32,2,128,128]{4,3,2,1,0:T(8,128)}, u32[]{:S(2)}) copy-start(f32[1,32,2,128,128]{4,3,2,1,0:T(8,128)} %param.6) | copy-start | bytes 12582916
  2.8 0.7 copy-start.2
  3.5 0.7 copy-start.5
  4.2 0.7 copy-start.6
  4.9 55.8 %copy-start.3 = (s32[2048]{0:T(1024)S(1)}, s32[2048]{0:T(1024)}, u32[]{:S(2)}) copy-start(s32[2048]{0:T(1024)} %param.9) | copy-start | bytes 24580
  4.9 55.8 %copy-start.4 = (s32[2048]{0:T(1024)S(1)}, s32[2048]{0:T(1024)}, u32[]{:S(2)}) copy-start(s32[2048]{0:T(1024)} %param.10) | copy-start | bytes 24580
  60.6 13.6 %copy-start.1 = (bf16[2048,128]{1,0:T(8,128)(2,1)S(1)}, bf16[2048,128]{1,0:T(8,128)(2,1)}, u32[]{:S(2)}) copy-start(bf16[2048,128]{1,0:T(8,128)(2,1)} %sketch.3) | copy-start | bytes 1572868

commit v3 on v2

--- a/solution.py
+++ b/solution.py
@@ -12,16 +12,19 @@
 RT_DEV = 16
 CT_DEV = 16
 NT = RT_DEV * CT_DEV
-HALF = TILE // 2
+LOW = 2
+CUTS = 8 // LOW
+CUT = TILE // CUTS
+MASK = 2**LOW - 1
 SHIFT = 0.25
-CODE = 1048570.0 / math.sqrt(30.0)
+CODE = (2.0 ** (16 + LOW) - 6.0) / math.sqrt(30.0)
 TOP = 32766.0
 MESH = pl.DeviceIdType.MESH
 MIB = 1024 * 1024
 
 
-def exchange_kernel(nr, nc, counts, places, used, row_tot, words_out, meta_out,
-                    send, meta, sem_s, sem_r, msem_s, msem_r, lsem):
+def exchange_kernel(nr, nc, source, places, used, row_tot, words_out, meta_out, row_inv,
+                    counts, send, meta, sem_s, sem_r, msem_s, msem_r, csem, lsem):
     n = nr * nc
     hr = nr // 2
     my_r = lax.axis_index("row")
@@ -38,10 +41,11 @@
             t = y * r
             t = t + 0.5 * r * (y - t * t)
             v = jnp.round(t * CODE).astype(jnp.int32)
-            send[o, h * TILE : (h + 1) * TILE] = ((v >> 4) - 32768).astype(jnp.int16)
-            v = v & 15
-            v = v[:HALF] + (v[HALF:] << 4)
-            low = v if h == 0 else low + (v << 8)
+            send[o, h * TILE : (h + 1) * TILE] = ((v >> LOW) - 32768).astype(jnp.int16)
+            v = v & MASK
+            for g in range(CUTS):
+                bits = v[g * CUT : (g + 1) * CUT] << (LOW * g + 8 * h)
+                low = bits if low is None else low + bits
         send[o, 2 * TILE :] = (low - 32768).astype(jnp.int16)
         k = jnp.where(lane == 2, used[0, o], part)
         k = jnp.where(lane == 1, places[1, o], k)
@@ -65,8 +69,20 @@
                 recv_sem=msem_r.at[i], device_id=(row, col), device_id_type=MESH),
         )
 
+    def load(i):
+        row, col = target(i)
+        o = row * nc + col
+        return pltpu.make_async_copy(source.at[o], counts.at[o], csem.at[i])
+
+    def fetch(i, _):
+        load(i).start()
+        return 0
+
+    lax.fori_loop(0, n, fetch, 0)
+
     def issue(i, _):
         o, (a, b) = copies(i)
+        load(i).wait()
         pack(o)
         a.start()
         b.start()
@@ -80,87 +96,86 @@
 
     issue(0, 0)
     lax.fori_loop(2, n, issue, 0)
+    load(1).wait()
     pack(me)
     own = pltpu.make_async_copy(send.at[me], words_out.at[me], lsem.at[0])
     own_meta = pltpu.make_async_copy(meta.at[me], meta_out.at[me], lsem.at[1])
     own.start()
     own_meta.start()
+
+    def rows(i, _):
+        r = 1.0 / row_tot[pl.ds(i, 1), :].astype(jnp.float32)
+        row_inv[pl.ds(i * TILE, TILE), :] = jnp.broadcast_to(r, (TILE, TILE)).T
+        return 0
+
+    lax.fori_loop(0, RT_DEV, rows, 0)
     finish(0, 0)
     lax.fori_loop(2, n, finish, 0)
     own.wait()
     own_meta.wait()
 
 
-def pmi_kernel(nr, nc, meta, words, row_tot, col_tot, out, acc, row_f, col_f, seen):
+def pmi_kernel(nr, nc, meta, words, row_inv, col_tot, out, acc, col_f, seen, held):
     n = nr * nc
 
     def clear(i, _):
-        seen[i] = 0
-        return 0
-
-    lax.fori_loop(0, NT, clear, 0)
+        for g in range(CT_DEV):
+            seen[i * CT_DEV + g] = 0
+        rs = pl.ds(pl.multiple_of(i * TILE, TILE), TILE)
+        out[rs, :] = jnp.zeros((TILE, CT_DEV * TILE), jnp.bfloat16)
+        return 0
+
+    lax.fori_loop(0, RT_DEV, clear, 0)
     total = lax.fori_loop(0, nr, lambda a, t: t + meta[a * nc, 0, 3], jnp.int32(0))
-    grand = total.astype(jnp.float32)
-    col_f[...] = (1.0 / (CODE * CODE)) / col_tot[...].astype(jnp.float32)
-
-    def rows(i, _):
-        r = row_tot[pl.ds(i, 1), :].astype(jnp.float32)
-        f = jnp.broadcast_to(grand / r, (TILE, TILE))
-        row_f[pl.ds(i * TILE, TILE), :] = f.T
-        return 0
-
-    lax.fori_loop(0, RT_DEV, rows, 0)
-
-    def add(s, _):
+    scale = total.astype(jnp.float32) * (1.0 / (CODE * CODE))
+    col_f[...] = scale / col_tot[...].astype(jnp.float32)
+
+    def add(s, count):
         for h in range(2):
             p = meta[s, 0, h]
-
-            @pl.when(h < meta[s, 0, 2])
+            valid = h < meta[s, 0, 2]
+            fresh = seen[p] == 0
+
+            def value(g):
+                low = (words[s, 2 * TILE :].astype(jnp.int32) + 32768) >> (LOW * g + 8 * h)
+                from_ = slice(h * TILE + g * CUT, h * TILE + (g + 1) * CUT)
+                v = (words[s, from_].astype(jnp.int32) + 32768) * (MASK + 1)
+                v = (v + (low & MASK)).astype(jnp.float32)
+                return v * v
+
+            @pl.when(jnp.logical_and(valid, fresh))
             def _():
-                low = (words[s, 2 * TILE :].astype(jnp.int32) + 32768) >> (8 * h)
-                fresh = seen[p] == 0
-                for g in range(2):
-                    at = slice(g * HALF, (g + 1) * HALF)
-                    from_ = slice(h * TILE + g * HALF, h * TILE + (g + 1) * HALF)
-                    v = (words[s, from_].astype(jnp.int32) + 32768) * 16
-                    v = (v + ((low >> (4 * g)) & 15)).astype(jnp.float32)
-                    v = v * v
-
-                    @pl.when(fresh)
-                    def _():
-                        acc[p, at] = v
-
-                    @pl.when(jnp.logical_not(fresh))
-                    def _():
-                        acc[p, at] = acc[p, at] + v
-
+                for g in range(CUTS):
+                    acc[p, g * CUT : (g + 1) * CUT] = value(g)
                 seen[p] = 1
-
-        return 0
-
-    lax.fori_loop(0, n, add, 0)
-
-    def tile(p, _):
+                held[count] = p
+
+            @pl.when(jnp.logical_and(valid, jnp.logical_not(fresh)))
+            def _():
+                for g in range(CUTS):
+                    at = slice(g * CUT, (g + 1) * CUT)
+                    acc[p, at] = acc[p, at] + value(g)
+
+            count = count + jnp.where(jnp.logical_and(valid, fresh), 1, 0)
+
+        return count
+
+    count = lax.fori_loop(0, n, add, jnp.int32(0))
+
+    def tile(i, _):
+        p = held[i]
         tr = p // CT_DEV
         tc = lax.rem(p, CT_DEV)
         rs = pl.ds(pl.multiple_of(tr * TILE, TILE), TILE)
         cs = pl.ds(pl.multiple_of(tc * TILE, TILE), TILE)
-
-        @pl.when(seen[p] == 0)
-        def _():
-            out[rs, cs] = jnp.zeros((TILE, TILE), jnp.bfloat16)
-
-        @pl.when(seen[p] != 0)
-        def _():
-            x = acc[p] * row_f[rs, :] * col_f[pl.ds(tc, 1), :]
-            out[rs, cs] = jnp.maximum(jnp.log(1.0 + x) - SHIFT, 0.0).astype(jnp.bfloat16)
-
-        return 0
-
-    lax.fori_loop(0, NT, tile, 0)
-
-
-def sketch_kernel(nr, nc, inv, pmi, sketch, rr_out, co_out, pa, ra, p1, r1, rr, acc, p2, r2,
+        x = acc[p] * row_inv[rs, :] * col_f[pl.ds(tc, 1), :]
+        out[rs, cs] = jnp.maximum(jnp.log(1.0 + x) - SHIFT, 0.0).astype(jnp.bfloat16)
+        return 0
+
+    lax.fori_loop(0, count, tile, 0)
+
+
+def sketch_kernel(nr, nc, inv, pmi, sketch, rr_out, co_out, pa, ra, p1, r1, rr, rt, own_co, p2, r2,
                   f2, g2, co, sas, sar, s1s, s1r, s2s, s2r, sfs, sfr, s3s, s3r, s5s, s5r,
                   s4s, s4r):
     my_r = lax.axis_index("row")
@@ -257,28 +272,37 @@
     lax.fori_loop(0, nk - 1, spread, 0)
     forward(0).start()
 
-    def turned(j):
-        left = rr[rows_of(j), :].astype(jnp.float32).T.astype(jnp.bfloat16)
-        return jnp.dot(left, pmi[rows_of(j), :], preferred_element_type=jnp.float32)
-
-    acc[...] = turned(my_c)
+    def turn(j):
+        block = rr[rows_of(j), :].astype(jnp.float32)
+        rt[:, rows_of(j)] = block.T.astype(jnp.bfloat16)
+
+    turn(my_c)
     forward(0).wait_recv()
-    acc[...] += turned(k * 2 + other)
+    turn(k * 2 + other)
 
     def second(i, _):
         d = i + 1
         ag_col(d).wait_recv()
         forward(d).start()
-        acc[...] += turned(origin(d) + core)
+        turn(origin(d) + core)
+        return 0
+
+    lax.fori_loop(0, nk - 1, second, 0)
+
+    def second_half(i, _):
+        d = i + 1
         forward(d).wait_recv()
-        acc[...] += turned(origin(d) + other)
-        return 0
-
-    lax.fori_loop(0, nk - 1, second, 0)
+        turn(origin(d) + other)
+        return 0
+
+    lax.fori_loop(0, nk - 1, second_half, 0)
+
+    def turned(j):
+        return jnp.dot(rt[...], pmi[:, cols_of(j)], preferred_element_type=jnp.float32)
 
     def third(i, _):
         d = i + 1
-        a = acc[:, cols_of(lax.rem(my_r + d, nr))]
+        a = turned(lax.rem(my_r + d, nr))
         m = jnp.max(jnp.abs(a), axis=0, keepdims=True)
         up = jnp.where(m > 1e-30, TOP / jnp.maximum(m, 1e-30), 0.0)
         p2[d] = jnp.round(a * up).astype(jnp.int32).astype(jnp.int16)
@@ -289,6 +313,7 @@
         return 0
 
     lax.fori_loop(0, nr - 1, third, 0)
+    own_co[...] = turned(my_r)
 
     def sent(i, _):
         d = i + 1
@@ -309,11 +334,11 @@
         a, b = rs_row(d)
         a.wait()
         b.wait()
-        acc[:, mine] += r2[d].astype(jnp.int32).astype(jnp.float32) * g2[d, 0:1, :]
+        own_co[...] += r2[d].astype(jnp.int32).astype(jnp.float32) * g2[d, 0:1, :]
         return 0
 
     lax.fori_loop(0, nr - 1, fourth, 0)
-    co[mine, :] = (acc[:, mine].T * inv).astype(jnp.bfloat16)
+    co[mine, :] = (own_co[...].T * inv).astype(jnp.bfloat16)
 
     def fifth(i, _):
         ag_row(i + 1).start()
@@ -337,36 +362,40 @@
     dma = pltpu.SemaphoreType.DMA
     f32, bf16, i16, i32 = jnp.float32, jnp.bfloat16, jnp.int16, jnp.int32
     row_tot = row_totals.reshape(RT_DEV, TILE)
-    words_rows = 2 * TILE + HALF
-    words, meta = pl.pallas_call(
+    words_rows = 2 * TILE + CUT
+    rows, cols = RT_DEV * TILE, CT_DEV * TILE
+    words, meta, row_inv = pl.pallas_call(
         functools.partial(exchange_kernel, nr, nc),
         out_shape=(
             jax.ShapeDtypeStruct((n, words_rows, TILE), i16),
             jax.ShapeDtypeStruct((n, 1, TILE), i32),
+            jax.ShapeDtypeStruct((rows, TILE), f32),
         ),
-        in_specs=[vm, sm, sm, vm],
-        out_specs=(hbm, hbm),
-        scratch_shapes=[pltpu.VMEM((n, words_rows, TILE), i16), pltpu.VMEM((n, 1, TILE), i32)]
-        + [dma((n,))] * 4 + [dma((2,))],
-        compiler_params=pltpu.CompilerParams(
-            has_side_effects=True, vmem_limit_bytes=8 * MIB + n * MIB // 4),
+        in_specs=[hbm, sm, sm, vm],
+        out_specs=(hbm, hbm, vm),
+        scratch_shapes=[
+            pltpu.VMEM((n, 2, TILE, TILE), f32),
+            pltpu.VMEM((n, words_rows, TILE), i16),
+            pltpu.VMEM((n, 1, TILE), i32),
+        ]
+        + [dma((n,))] * 5 + [dma((2,))],
+        compiler_params=pltpu.CompilerParams(has_side_effects=True, vmem_limit_bytes=56 * MIB),
         name="exchange",
     )(pair_counts[0], tile_index[0].T, slot_counts, row_tot)
     pmi = pl.pallas_call(
         functools.partial(pmi_kernel, nr, nc),
-        out_shape=jax.ShapeDtypeStruct((RT_DEV * TILE, CT_DEV * TILE), bf16),
+        out_shape=jax.ShapeDtypeStruct((rows, cols), bf16),
         in_specs=[sm, vm, vm, vm],
         out_specs=vm,
         scratch_shapes=[
             pltpu.VMEM((NT, TILE, TILE), f32),
-            pltpu.VMEM((RT_DEV * TILE, TILE), f32),
             pltpu.VMEM((CT_DEV, TILE), f32),
+            pltpu.SMEM((NT,), i32),
             pltpu.SMEM((NT,), i32),
         ],
         compiler_params=pltpu.CompilerParams(vmem_limit_bytes=30 * MIB + n * MIB // 10),
         name="pmi",
-    )(meta, words, row_tot, col_totals.reshape(CT_DEV, TILE))
-    rows, cols = pmi.shape
+    )(meta, words, row_inv, col_totals.reshape(CT_DEV, TILE))
     sk = sketch.shape[1]
     ch, cz, nk = rows // nc, cols // nr, nc // 2
     return pl.pallas_call(
@@ -380,7 +409,8 @@
         scratch_shapes=[pltpu.VMEM((nk, ch, sk), f32)] * 4
         + [
             pltpu.VMEM((rows, sk), bf16),
-            pltpu.VMEM((sk, cols), f32),
+            pltpu.VMEM((sk, rows), bf16),
+            pltpu.VMEM((sk, cz), f32),
             pltpu.VMEM((nr, sk, cz), i16),
             pltpu.VMEM((nr, sk, cz), i16),
             pltpu.VMEM((nr, 8, cz), f32),

time: 139 us -> 126 us (0.906)
  Pallas kernels: 132 us -> 119 us
    pallas_call x1, Pallas kernels: 13.5 us -> 4.6 us  [on_device(): pl.pallas_call(functools.partial(pmi_kernel, nr, nc), out_shape=jax.Shape...]
    pallas_call x1, Pallas kernels: 62.3 us -> 60.4 us  [on_device(): pl.pallas_call(functools.partial(sketch_kernel, nr, nc, 1.0 / math.sqrt(r...]
    pallas_call x1, Pallas kernels: 55.8 us -> 54.1 us  [on_device(): pl.pallas_call(functools.partial(exchange_kernel, nr, nc), out_shape=(jax...]
    unnamed x16 -> x12, local copies, waits for them, and re-layouts: 5.81 us -> 5.2 us
where the time goes in v3:
time: 126 us; the launch traced here: 125 us
  Pallas kernels  119 us (94%)
  local copies, waits for them, and re-layouts  5.2 us (4%)
    pallas_call x1, Pallas kernels, on_device(): pl.pallas_call(functools.partial(sketch_kernel, nr, nc, 1.0 / math.sqrt(r...  60.4 us
    pallas_call x1, Pallas kernels, on_device(): pl.pallas_call(functools.partial(exchange_kernel, nr, nc), out_shape=(jax...  54.1 us
    unnamed x12, local copies, waits for them, and re-layouts  5.2 us
    pallas_call x1, Pallas kernels, on_device(): pl.pallas_call(functools.partial(pmi_kernel, nr, nc), out_shape=jax.Shape...  4.6 us

profile of v3, /device:TPU:0, one launch (start us, length us, event | category | flops | bytes accessed | tf_op | source)
XLA Modules:
  0.0 124.9 jit_solution(5464051522129939307)
XLA Ops:
  0.6 0.0 copy-start.4
  0.6 54.1 %exchange.1 = (s16[32,288,128]{2,1,0:T(8,128)(2,1)}, s32[32,1,128]{2,1,0:T(1,128)}, f32[2048,128]{1,0:T(8,128)}) custom-call(f32[32,2,128,128]{3,2,1,0:T(8,128)} %bitcast.7, s32[2,32]{1,0:T(2,128)} %bitcast.9, s32[1,32]{1,0:T(1,128)} %used.1, s32[16,128]{1,0:T(8,128)} %bitcast.8), custom_call_target="tpu_custom_call" | custom-call | tf_op jit(solution)/shard_map/exchange/pallas_call | solution.py:367
  54.7 0.0 copy-done.4
  54.7 0.0 copy-start
  54.8 1.7 %copy-done = s16[32,288,128]{2,1,0:T(8,128)(2,1)S(1)} copy-done((s16[32,288,128]{2,1,0:T(8,128)(2,1)S(1)}, s16[32,288,128]{2,1,0:T(8,128)(2,1)}, u32[]{:S(2)}) %copy-start) | copy-done | bytes 2359320
  56.4 0.0 copy-start.1
  56.4 1.2 copy-done.1
  57.6 0.0 copy-start.3
  57.6 0.7 copy-done.3
  58.4 0.0 copy-start.2
  58.4 4.6 %pmi.1 = bf16[2048,2048]{1,0:T(8,128)(2,1)S(1)} custom-call(s32[32,1,128]{2,1,0:T(1,128)S(1)} %copy-done.3, s16[32,288,128]{2,1,0:T(8,128)(2,1)S(1)} %copy-done, f32[2048,128]{1,0:T(8,128)S(1)} %copy-done.1, s32[16,128]{1,0:T(8,128)S(1)} %bitcast.6), custom_call_target="tpu_custom_call" | custom-call | tf_op jit(solution)/shard_map/pmi/pallas_call | solution.py:385
  63.0 0.0 copy-done.2
  63.0 60.4 %sketch.2 = (bf16[2048,128]{1,0:T(8,128)(2,1)S(1)}, bf16[2048,128]{1,0:T(8,128)(2,1)S(1)}) custom-call(bf16[2048,2048]{1,0:T(8,128)(2,1)S(1)} %pmi.1, bf16[2048,128]{1,0:T(8,128)(2,1)S(1)} %copy-done.2), custom_call_target="tpu_custom_call" | custom-call | tf_op jit(solution)/shard_map/sketch/pallas_call | solution.py:401
  123.4 0.8 copy.10
  124.1 0.8 copy.11
Async XLA Ops:
  0.6 54.1 %copy-start.4 = (s32[2048]{0:T(1024)S(1)}, s32[2048]{0:T(1024)}, u32[]{:S(2)}) copy-start(s32[2048]{0:T(1024)} %param.10) | copy-start | bytes 24580
  54.7 1.7 %copy-start = (s16[32,288,128]{2,1,0:T(8,128)(2,1)S(1)}, s16[32,288,128]{2,1,0:T(8,128)(2,1)}, u32[]{:S(2)}) copy-start(s16[32,288,128]{2,1,0:T(8,128)(2,1)} %get-tuple-element.6.words) | copy-start | bytes 7077892
  56.4 1.2 copy-start.1
  57.6 0.7 copy-start.3
  58.4 4.6 %copy-start.2 = (bf16[2048,128]{1,0:T(8,128)(2,1)S(1)}, bf16[2048,128]{1,0:T(8,128)(2,1)}, u32[]{:S(2)}) copy-start(bf16[2048,128]{1,0:T(8,128)(2,1)} %sketch.3) | copy-start | bytes 1572868

commit v4 on v3

--- a/solution.py
+++ b/solution.py
@@ -17,7 +17,8 @@
 CUT = TILE // CUTS
 MASK = 2**LOW - 1
 SHIFT = 0.25
-CODE = (2.0 ** (16 + LOW) - 6.0) / math.sqrt(30.0)
+CODE = (2.0 ** (16 + LOW) - 10.0) / (30.0**0.25 - 0.01**0.25)
+BASE = math.floor(0.01**0.25 * CODE) - 4
 TOP = 32766.0
 MESH = pl.DeviceIdType.MESH
 MIB = 1024 * 1024
@@ -33,14 +34,16 @@
     part = jnp.sum(row_tot[...])
     lane = lax.broadcasted_iota(jnp.int32, (1, TILE), 1)
 
+    def root(y):
+        r = lax.rsqrt(y)
+        t = y * r
+        return t + 0.5 * r * (y - t * t)
+
     def pack(o):
         low = None
         for h in range(2):
-            y = counts[o, h]
-            r = lax.rsqrt(y)
-            t = y * r
-            t = t + 0.5 * r * (y - t * t)
-            v = jnp.round(t * CODE).astype(jnp.int32)
+            t = root(root(counts[o, h]))
+            v = jnp.round(t * CODE - BASE).astype(jnp.int32)
             send[o, h * TILE : (h + 1) * TILE] = ((v >> LOW) - 32768).astype(jnp.int16)
             v = v & MASK
             for g in range(CUTS):
@@ -127,8 +130,7 @@
 
     lax.fori_loop(0, RT_DEV, clear, 0)
     total = lax.fori_loop(0, nr, lambda a, t: t + meta[a * nc, 0, 3], jnp.int32(0))
-    scale = total.astype(jnp.float32) * (1.0 / (CODE * CODE))
-    col_f[...] = scale / col_tot[...].astype(jnp.float32)
+    col_f[...] = total.astype(jnp.float32) / col_tot[...].astype(jnp.float32)
 
     def add(s, count):
         for h in range(2):
@@ -140,7 +142,8 @@
                 low = (words[s, 2 * TILE :].astype(jnp.int32) + 32768) >> (LOW * g + 8 * h)
                 from_ = slice(h * TILE + g * CUT, h * TILE + (g + 1) * CUT)
                 v = (words[s, from_].astype(jnp.int32) + 32768) * (MASK + 1)
-                v = (v + (low & MASK)).astype(jnp.float32)
+                v = (v + (low & MASK) + BASE).astype(jnp.float32) * (1.0 / CODE)
+                v = v * v
                 return v * v
 
             @pl.when(jnp.logical_and(valid, fresh))
@@ -235,6 +238,18 @@
 
     def product(j):
         return jnp.dot(pmi[rows_of(j), :], sketch[...], preferred_element_type=jnp.float32)
+
+    barrier = pltpu.get_barrier_semaphore()
+
+    def greet(to):
+        pl.semaphore_signal(barrier, inc=1, device_id=to, device_id_type=MESH)
+
+    greet(sibling)
+    for d in range(1, nk):
+        greet(chip(d))
+    for d in range(1, nr):
+        greet(row_peer(d))
+    pl.semaphore_wait(barrier, nk + nr - 1)
 
     def zeroth(i, _):
         d = lax.rem(i + 1, nk)
@@ -379,7 +394,7 @@
             pltpu.VMEM((n, 1, TILE), i32),
         ]
         + [dma((n,))] * 5 + [dma((2,))],
-        compiler_params=pltpu.CompilerParams(has_side_effects=True, vmem_limit_bytes=56 * MIB),
+        compiler_params=pltpu.CompilerParams(has_side_effects=True, vmem_limit_bytes=48 * MIB),
         name="exchange",
     )(pair_counts[0], tile_index[0].T, slot_counts, row_tot)
     pmi = pl.pallas_call(
@@ -418,7 +433,8 @@
             pltpu.VMEM((cols, sk), bf16),
         ]
         + [dma((nk,))] * 8 + [dma((nr,))] * 6,
-        compiler_params=pltpu.CompilerParams(has_side_effects=True, vmem_limit_bytes=24 * MIB),
+        compiler_params=pltpu.CompilerParams(
+            has_side_effects=True, vmem_limit_bytes=24 * MIB, collective_id=1),
         name="sketch",
     )(pmi, sketch)
 

time: 126 us -> 120 us (0.952)
  Pallas kernels: 119 us -> 115 us
  local copies, waits for them, and re-layouts: 5.2 us -> 3.62 us
    pallas_call x1, Pallas kernels: 60.4 us -> 57.2 us  [on_device(): pl.pallas_call(functools.partial(sketch_kernel, nr, nc, 1.0 / math.sqrt(r...]
    unnamed x12, local copies, waits for them, and re-layouts: 5.2 us -> 3.62 us
where the time goes in v4:
time: 120 us; the launch traced here: 119 us
  Pallas kernels  115 us (96%)
  local copies, waits for them, and re-layouts  3.62 us (3%)
    pallas_call x1, Pallas kernels, on_device(): pl.pallas_call(functools.partial(sketch_kernel, nr, nc, 1.0 / math.sqrt(r...  57.2 us
    pallas_call x1, Pallas kernels, on_device(): pl.pallas_call(functools.partial(exchange_kernel, nr, nc), out_shape=(jax...  52.9 us
    pallas_call x1, Pallas kernels, on_device(): pl.pallas_call(functools.partial(pmi_kernel, nr, nc), out_shape=jax.Shape...  4.68 us
    unnamed x12, local copies, waits for them, and re-layouts  3.62 us

profile of v4, /device:TPU:0, one launch (start us, length us, event | category | flops | bytes accessed | tf_op | source)
XLA Modules:
  0.0 119.1 jit_solution(5227450856362598745)
XLA Ops:
  0.6 0.0 copy-start.1
  0.6 0.7 copy-done.1
  1.3 0.0 copy-start.3
  1.3 0.7 copy-done.3
  2.0 0.0 copy-start.4
  2.0 0.7 copy-done.4
  2.7 0.0 copy-start.2
  2.7 52.9 %exchange.1 = (s16[32,288,128]{2,1,0:T(8,128)(2,1)S(1)}, s32[32,1,128]{2,1,0:T(1,128)S(1)}, f32[2048,128]{1,0:T(8,128)S(1)}) custom-call(f32[32,2,128,128]{3,2,1,0:T(8,128)} %bitcast.9, s32[2,32]{1,0:T(2,128)S(1)} %bitcast.8, s32[1,32]{1,0:T(1,128)S(1)} %copy-done.4, s32[16,128]{1,0:T(8,128)S(1)} %bitcast.6), custom_call_target="tpu_custom_call" | custom-call | tf_op jit(solution)/shard_map/exchange/pallas_call | solution.py:382
  55.6 0.0 copy-done.2
  55.6 0.0 copy-start
  55.6 4.7 %pmi.1 = bf16[2048,2048]{1,0:T(8,128)(2,1)S(1)} custom-call(s32[32,1,128]{2,1,0:T(1,128)S(1)} %get-tuple-element.5.meta, s16[32,288,128]{2,1,0:T(8,128)(2,1)S(1)} %get-tuple-element.6.words, f32[2048,128]{1,0:T(8,128)S(1)} %get-tuple-element.7.row_inv, s32[16,128]{1,0:T(8,128)S(1)} %bitcast.7), custom_call_target="tpu_custom_call" | custom-call | tf_op jit(solution)/shard_map/pmi/pallas_call | solution.py:400
  60.3 0.0 copy-done
  60.3 57.2 %sketch.2 = (bf16[2048,128]{1,0:T(8,128)(2,1)S(1)}, bf16[2048,128]{1,0:T(8,128)(2,1)S(1)}) custom-call(bf16[2048,2048]{1,0:T(8,128)(2,1)S(1)} %pmi.1, bf16[2048,128]{1,0:T(8,128)(2,1)S(1)} %copy-done), custom_call_target="tpu_custom_call" | custom-call | tf_op jit(solution)/shard_map/sketch/pallas_call | solution.py:416
  117.5 0.8 copy.10
  118.3 0.8 copy.11
Async XLA Ops:
  0.6 0.7 copy-start.1
  1.3 0.7 copy-start.3
  2.0 0.7 copy-start.4
  2.7 52.9 %copy-start.2 = (s32[2048]{0:T(1024)S(1)}, s32[2048]{0:T(1024)}, u32[]{:S(2)}) copy-start(s32[2048]{0:T(1024)} %param.10) | copy-start | bytes 24580
  55.6 4.7 %copy-start = (bf16[2048,128]{1,0:T(8,128)(2,1)S(1)}, bf16[2048,128]{1,0:T(8,128)(2,1)}, u32[]{:S(2)}) copy-start(bf16[2048,128]{1,0:T(8,128)(2,1)} %sketch.3) | copy-start | bytes 1572868

commit v5 on v4

--- a/solution.py
+++ b/solution.py
@@ -180,7 +180,7 @@
 
 def sketch_kernel(nr, nc, inv, pmi, sketch, rr_out, co_out, pa, ra, p1, r1, rr, rt, own_co, p2, r2,
                   f2, g2, co, sas, sar, s1s, s1r, s2s, s2r, sfs, sfr, s3s, s3r, s5s, s5r,
-                  s4s, s4r):
+                  s4s, s4r, s6s, s6r):
     my_r = lax.axis_index("row")
     my_c = lax.axis_index("col")
     nk = nc // 2
@@ -232,10 +232,6 @@
             remote(f2.at[d], g2.at[d], s5s.at[d], s5r.at[d], row_peer(d)),
         )
 
-    def ag_row(d):
-        mine = co.at[cols_of(my_r)]
-        return remote(mine, mine, s4s.at[d], s4r.at[d], row_peer(d))
-
     def product(j):
         return jnp.dot(pmi[rows_of(j), :], sketch[...], preferred_element_type=jnp.float32)
 
@@ -355,17 +351,61 @@
     lax.fori_loop(0, nr - 1, fourth, 0)
     co[mine, :] = (own_co[...].T * inv).astype(jnp.bfloat16)
 
+    up_ok = my_r < nr - 1
+    down_ok = my_r > 0
+
+    def ag_up(j):
+        block = co.at[cols_of(j)]
+        return remote(block, block, s4s.at[j], s4r.at[j], row_peer(1))
+
+    def ag_down(j):
+        block = co.at[cols_of(j)]
+        return remote(block, block, s6s.at[j], s6r.at[j], row_peer(nr - 1))
+
+    @pl.when(up_ok)
+    def _():
+        ag_up(my_r).start()
+
+    @pl.when(down_ok)
+    def _():
+        ag_down(my_r).start()
+
     def fifth(i, _):
-        ag_row(i + 1).start()
+        low = my_r - 1 - i
+        high = my_r + 1 + i
+
+        @pl.when(low >= 0)
+        def _():
+            ag_up(low).wait_recv()
+
+            @pl.when(up_ok)
+            def _():
+                ag_up(low).start()
+
+        @pl.when(high < nr)
+        def _():
+            ag_down(high).wait_recv()
+
+            @pl.when(down_ok)
+            def _():
+                ag_down(high).start()
+
         return 0
 
     lax.fori_loop(0, nr - 1, fifth, 0)
 
-    def sixth(i, _):
-        ag_row(i + 1).wait()
-        return 0
-
-    lax.fori_loop(0, nr - 1, sixth, 0)
+    def sixth(j, _):
+        @pl.when(jnp.logical_and(up_ok, j <= my_r))
+        def _():
+            ag_up(j).wait_send()
+
+        @pl.when(jnp.logical_and(down_ok, j >= my_r))
+        def _():
+            ag_down(j).wait_send()
+
+        return 0
+
+    lax.fori_loop(0, nr, sixth, 0)
     co_out[...] = co[...]
 
 
@@ -432,7 +472,7 @@
             pltpu.VMEM((nr, 8, cz), f32),
             pltpu.VMEM((cols, sk), bf16),
         ]
-        + [dma((nk,))] * 8 + [dma((nr,))] * 6,
+        + [dma((nk,))] * 8 + [dma((nr,))] * 8,
         compiler_params=pltpu.CompilerParams(
             has_side_effects=True, vmem_limit_bytes=24 * MIB, collective_id=1),
         name="sketch",

time: 120 us -> 123 us (1.025)
  Pallas kernels: 115 us -> 118 us
    pallas_call x1, Pallas kernels: 57.2 us -> 60.4 us  [on_device(): pl.pallas_call(functools.partial(sketch_kernel, nr, nc, 1.0 / math.sqrt(r...]
where the time goes in v5:
time: 123 us
  Pallas kernels  118 us (96%)
  local copies, waits for them, and re-layouts  3.62 us (3%)
    pallas_call x1, Pallas kernels, on_device(): pl.pallas_call(functools.partial(sketch_kernel, nr, nc, 1.0 / math.sqrt(r...  60.4 us
    pallas_call x1, Pallas kernels, on_device(): pl.pallas_call(functools.partial(exchange_kernel, nr, nc), out_shape=(jax...  52.9 us
    pallas_call x1, Pallas kernels, on_device(): pl.pallas_call(functools.partial(pmi_kernel, nr, nc), out_shape=jax.Shape...  5.03 us
    unnamed x12, local copies, waits for them, and re-layouts  3.62 us

profile of v5, /device:TPU:0, one launch (start us, length us, event | category | flops | bytes accessed | tf_op | source)
XLA Modules:
  0.0 122.6 jit_solution(805820735396570849)
XLA Ops:
  0.6 0.0 copy-start.1
  0.6 0.7 copy-done.1
  1.3 0.0 copy-start.3
  1.3 0.7 copy-done.3
  2.0 0.0 copy-start.4
  2.0 0.7 copy-done.4
  2.7 0.0 copy-start.2
  2.7 52.9 %exchange.1 = (s16[32,288,128]{2,1,0:T(8,128)(2,1)S(1)}, s32[32,1,128]{2,1,0:T(1,128)S(1)}, f32[2048,128]{1,0:T(8,128)S(1)}) custom-call(f32[32,2,128,128]{3,2,1,0:T(8,128)} %bitcast.9, s32[2,32]{1,0:T(2,128)S(1)} %bitcast.8, s32[1,32]{1,0:T(1,128)S(1)} %copy-done.4, s32[16,128]{1,0:T(8,128)S(1)} %bitcast.6), custom_call_target="tpu_custom_call" | custom-call | tf_op jit(solution)/shard_map/exchange/pallas_call | solution.py:422
  55.6 0.0 copy-done.2
  55.6 0.0 copy-start
  55.6 5.0 %pmi.1 = bf16[2048,2048]{1,0:T(8,128)(2,1)S(1)} custom-call(s32[32,1,128]{2,1,0:T(1,128)S(1)} %get-tuple-element.5.meta, s16[32,288,128]{2,1,0:T(8,128)(2,1)S(1)} %get-tuple-element.6.words, f32[2048,128]{1,0:T(8,128)S(1)} %get-tuple-element.7.row_inv, s32[16,128]{1,0:T(8,128)S(1)} %bitcast.7), custom_call_target="tpu_custom_call" | custom-call | tf_op jit(solution)/shard_map/pmi/pallas_call | solution.py:440
  60.6 0.0 copy-done
  60.6 60.4 %sketch.2 = (bf16[2048,128]{1,0:T(8,128)(2,1)S(1)}, bf16[2048,128]{1,0:T(8,128)(2,1)S(1)}) custom-call(bf16[2048,2048]{1,0:T(8,128)(2,1)S(1)} %pmi.1, bf16[2048,128]{1,0:T(8,128)(2,1)S(1)} %copy-done), custom_call_target="tpu_custom_call" | custom-call | tf_op jit(solution)/shard_map/sketch/pallas_call | solution.py:456
  121.0 0.8 copy.10
  121.8 0.8 copy.11
Async XLA Ops:
  0.6 0.7 copy-start.1
  1.3 0.7 copy-start.3
  2.0 0.7 copy-start.4
  2.7 52.9 %copy-start.2 = (s32[2048]{0:T(1024)S(1)}, s32[2048]{0:T(1024)}, u32[]{:S(2)}) copy-start(s32[2048]{0:T(1024)} %param.10) | copy-start | bytes 24580
  55.6 5.1 %copy-start = (bf16[2048,128]{1,0:T(8,128)(2,1)S(1)}, bf16[2048,128]{1,0:T(8,128)(2,1)}, u32[]{:S(2)}) copy-start(bf16[2048,128]{1,0:T(8,128)(2,1)} %sketch.3) | copy-start | bytes 1572868
